TPU v7x, 32 devices: a whole 2x2x4 slice. The times are simulated.
32 devices in a mesh: groups: 2 (over x), seq: 16 (over z, y, core).
Axes of the slice: x: 2, y: 2, z: 4, core: 2. Of those that a mesh axis runs over, the one named last changes fastest.
Arguments:
- q_rows: bfloat16 [4096, 2048], P(('groups', 'seq')), parts along dimension 0, may hold values from -6 to 6
- k_rows: bfloat16 [4096, 2048], P(('groups', 'seq')), parts along dimension 0, may hold values from -6 to 6
- v_rows: bfloat16 [4096, 2048], P(('groups', 'seq')), parts along dimension 0, may hold values from -6 to 6
- block_of: int32 [4096, 1], P(('groups', 'seq')), parts along dimension 0, may hold values from 0 to 15; in each aligned block of 128 rows (0 to 127, 128 to 255, ...) at most 12 rows name the same one
- modality: int32 [4096], P(('groups', 'seq')), parts along dimension 0, may hold values from 0 to 2
- out_gain: float32 [3, 2048], replicated, may hold values from 0.1 to 1.9
Outputs:
- mixed: bfloat16 [4096, 2048], P(('groups', 'seq')), parts along dimension 0
There are 2 independent parts, one for each index of `groups`. A program takes and returns all parts, laid end to end along the dimension named above; an argument that names none is the same for every part. Nothing has to cross between parts.
Inputs may be any that keep to these rules, and one draw needn't show every extreme that they name: `block_of`: among the rows of one device no block is named more than 12 times, and some block is named exactly 12 times by the rows of some device.
All inputs are finite; a program needn't handle non-finite values.
Results may differ from a plain program's by a relative error of at most 0.0057.
Values may be sent and summed in bfloat16 or wider, within the bound.
A program may use at most 192 MiB of HBM per device.

v0:
```python
import math

import jax
import jax.numpy as jnp
from jax import lax
from jax.sharding import PartitionSpec as P

HEADS = 16
HEAD_DIM = 128


def entering(part, axis, combine, identity):
    place = lax.axis_index(axis)
    gathered = lax.all_gather(part, axis)
    state = jnp.zeros_like(part) + jnp.asarray(identity, part.dtype)

    def one(lap, state):
        return combine(state, lax.dynamic_index_in_dim(gathered, lap, 0, False))

    return lax.fori_loop(0, place, one, state)


def block_state(key_rows, value_rows):
    return jnp.einsum("shd,she->hde", key_rows, value_rows, preferred_element_type=jnp.float32)


def add_states(earlier, later):
    return earlier + later


def attend(queries, row_order, key_rows, value_rows, carried):
    row_count = queries.shape[0]
    head_count = queries.shape[1]
    slot_count = key_rows.shape[0]
    group_size = math.gcd(head_count, 4)
    carried_part = jnp.einsum("rhd,hde->rhe", queries, carried, preferred_element_type=jnp.float32)
    causal = row_order[:, None] >= jnp.arange(slot_count, dtype=jnp.int32)[None, :]

    def one_group(group_id):
        query_group = lax.dynamic_slice_in_dim(queries, group_id * group_size, group_size, 1)
        key_group = lax.dynamic_slice_in_dim(key_rows, group_id * group_size, group_size, 1)
        value_group = lax.dynamic_slice_in_dim(value_rows, group_id * group_size, group_size, 1)
        scores = jnp.einsum(
            "rhd,shd->hrs", query_group, key_group, preferred_element_type=jnp.float32
        )
        weights = jnp.where(causal[None], scores, 0.0).astype(jnp.bfloat16)
        return jnp.einsum("hrs,she->rhe", weights, value_group, preferred_element_type=jnp.float32)

    pieces = lax.map(one_group, jnp.arange(head_count // group_size, dtype=jnp.int32))
    local_part = jnp.moveaxis(pieces, 0, 1).reshape(row_count, head_count, queries.shape[2])
    combined = carried_part + local_part
    scale = lax.rsqrt(jnp.mean(combined * combined, axis=-1, keepdims=True) + 1e-06)
    return (combined * scale).astype(jnp.bfloat16)


def on_device(q_rows, k_rows, v_rows, block_of, modality, out_gain):
    tok_count = q_rows.shape[0]
    row_width = q_rows.shape[1]
    peer_count = lax.axis_size("seq")
    capacity = max(2, 3 * tok_count // (2 * peer_count))
    slot_count = peer_count * capacity
    head_count = HEADS
    head_size = HEAD_DIM
    target = block_of[:, 0]
    member = (target[:, None] == jnp.arange(peer_count, dtype=jnp.int32)[None, :]).astype(jnp.int32)
    slot_rank = jnp.sum((jnp.cumsum(member, axis=0) - 1) * member, axis=1)
    slot_index = target * capacity + slot_rank

    def packed(row_block):
        buffer = jnp.zeros((slot_count, row_width), row_block.dtype).at[slot_index].set(row_block)
        return buffer.reshape(peer_count, capacity, row_width)

    q_send = packed(q_rows)
    k_send = packed(k_rows)
    v_send = packed(v_rows)
    q_recv, k_recv, v_recv = (
        lax.all_to_all(q_send, "seq", split_axis=0, concat_axis=0, tiled=True),
        lax.all_to_all(k_send, "seq", split_axis=0, concat_axis=0, tiled=True),
        lax.all_to_all(v_send, "seq", split_axis=0, concat_axis=0, tiled=True),
    )
    key_rows = k_recv.reshape(slot_count, head_count, head_size)
    value_rows = v_recv.reshape(slot_count, head_count, head_size)
    block_sum = block_state(key_rows, value_rows)
    prefix = entering(block_sum, "seq", add_states, jnp.zeros_like(block_sum))
    carried = prefix.astype(jnp.bfloat16)
    queries = q_recv.reshape(slot_count, head_count, head_size)
    normed = attend(queries, jnp.arange(slot_count, dtype=jnp.int32), key_rows, value_rows, carried)
    returned = lax.all_to_all(
        normed.reshape(peer_count, capacity, row_width),
        "seq",
        split_axis=0,
        concat_axis=0,
        tiled=True,
    )
    own_rows = returned.reshape(slot_count, row_width)[slot_index]
    chosen = modality[:, None]
    gains = jnp.where(
        chosen == 0,
        out_gain[0][None, :],
        jnp.where(chosen == 1, out_gain[1][None, :], out_gain[2][None, :]),
    )
    return (own_rows.astype(jnp.float32) * gains).astype(jnp.bfloat16)


def solution(mesh):
    placed = (
        P(("groups", "seq"), None),
        P(("groups", "seq"), None),
        P(("groups", "seq"), None),
        P(("groups", "seq"), None),
        P(("groups", "seq")),
        P(),
    )
    return jax.shard_map(
        on_device, mesh=mesh, in_specs=placed, out_specs=P(("groups", "seq"), None), check_vma=False
    )
```

profile of v0, /device:TPU:0, one launch (start us, length us, event | category | flops | bytes accessed | tf_op | source)
XLA Modules:
  0.0 286.4 jit_solution(9544114790081609818)
XLA Ops:
  6.5 0.7 fusion.23
  7.3 0.2 reduce_window_sum.11
  7.4 0.8 select_reduce_fusion
  8.3 0.7 fusion.24
  8.9 2.1 scatter_custom_fusion
  11.1 1.2 reshape.43
  12.3 7.4 %all-to-all-start = ((bf16[16,12,2048]{2,1,0:T(8,128)(2,1)}), bf16[16,12,2048]{2,1,0:T(8,128)(2,1)S(1)}, u32[]{:S(2)}, u32[]{:S(2)}) async-start(bf16[16,12,2048]{2,1,0:T(8,128)(2,1)} %reshape.43), calls=%async_computation | async-start | bytes 2097152 | tf_op jit(solution)/shard_map/all_to_all | solution.py:78
  19.6 2.1 scatter_custom_fusion.1
  21.8 1.1 reshape.45
  22.9 19.7 %all-to-all-done = bf16[16,12,2048]{2,1,0:T(8,128)(2,1)S(1)} async-done(((bf16[16,12,2048]{2,1,0:T(8,128)(2,1)}), bf16[16,12,2048]{2,1,0:T(8,128)(2,1)S(1)}, u32[]{:S(2)}, u32[]{:S(2)}) %all-to-all-start) | async-done | bytes 786464 | tf_op jit(solution)/shard_map/all_to_all | solution.py:78
  42.6 6.9 %all-to-all-start.1 = ((bf16[16,12,2048]{2,1,0:T(8,128)(2,1)}), bf16[16,12,2048]{2,1,0:T(8,128)(2,1)S(1)}, u32[]{:S(2)}, u32[]{:S(2)}) async-start(bf16[16,12,2048]{2,1,0:T(8,128)(2,1)} %reshape.45), calls=%async_computation.1 | async-start | bytes 2097152 | tf_op jit(solution)/shard_map/all_to_all | solution.py:79
  49.5 0.0 all-gather.3.cloned.1.call-start
  49.5 0.6 reshape.44
  50.1 22.3 %all-to-all-done.1 = bf16[16,12,2048]{2,1,0:T(8,128)(2,1)S(1)} async-done(((bf16[16,12,2048]{2,1,0:T(8,128)(2,1)}), bf16[16,12,2048]{2,1,0:T(8,128)(2,1)S(1)}, u32[]{:S(2)}, u32[]{:S(2)}) %all-to-all-start.1) | async-done | bytes 786464 | tf_op jit(solution)/shard_map/all_to_all | solution.py:79
  72.4 0.6 reshape.46
  73.0 1.5 fusion.26
  74.4 0.0 all-gather.3.cloned.1.call-update
  74.5 2.1 scatter_custom_fusion.2
  76.6 1.2 reshape.47
  77.8 6.9 %all-to-all-start.2 = ((bf16[16,12,2048]{2,1,0:T(8,128)(2,1)}), bf16[16,12,2048]{2,1,0:T(8,128)(2,1)S(1)}, u32[]{:S(2)}, u32[]{:S(2)}) async-start(bf16[16,12,2048]{2,1,0:T(8,128)(2,1)} %reshape.47), calls=%async_computation.2 | async-start | bytes 2097152 | tf_op jit(solution)/shard_map/all_to_all | solution.py:77
  84.6 0.2 copy.14
  84.9 1.1 copy.15
  85.9 38.2 %all-to-all-done.2 = bf16[16,12,2048]{2,1,0:T(8,128)(2,1)S(1)} async-done(((bf16[16,12,2048]{2,1,0:T(8,128)(2,1)}), bf16[16,12,2048]{2,1,0:T(8,128)(2,1)S(1)}, u32[]{:S(2)}, u32[]{:S(2)}) %all-to-all-start.2) | async-done | bytes 786464 | tf_op jit(solution)/shard_map/all_to_all | solution.py:77
  124.2 0.6 reshape.48
  124.7 0.2 copy.16
  124.9 13.9 %while.22 = (s32[]{:T(128)}, f32[4,192,4,128]{3,1,2,0:T(8,128)}, s32[4]{0:T(128)S(1)}, bf16[192,16,128]{2,0,1:T(8,128)(2,1)}, bf16[192,16,128]{2,0,1:T(8,128)(2,...) while((s32[]{:T(128)}, f32[4,192,4,128]{3,1,2,0:T(8,128)}, ...), condition=%wide.region_8.9_spmd.clone, body=%wide.region_7.8_spmd.clone.sunk | while | flops 75829256 | bytes 1071263 | solution.py:49
  125.0 0.7 dynamic_slice.39
  126.3 2.1 fusion.37
  128.4 0.7 dynamic_slice.39
  129.8 2.1 fusion.37
  131.9 0.7 dynamic_slice.39
  133.3 2.1 fusion.37
  135.4 0.7 dynamic_slice.39
  136.8 2.1 fusion.37
  138.9 86.5 %all-gather.3.cloned.1.call-done = f32[256,128,128]{2,1,0:T(8,128)} async-done(((f32[16,128,128]{2,1,0:T(8,128)}), f32[256,128,128]{2,1,0:T(8,128)}) %all-gather.3.cloned.1.call-update) | async-done | bytes 16777232 | tf_op jit(solution)/shard_map/all_gather | solution.py:14
  225.4 0.1 broadcast_in_dim.78
  225.5 1.4 copy-done
  226.9 0.4 bitcast_add_fusion.1
  227.3 0.6 multiply_reduce_fusion
  227.9 0.5 multiply_convert_fusion
  228.4 0.5 copy.20
  228.9 0.0 copy-start.1
  228.9 1.5 reshape.50
  230.4 24.0 %all-to-all-start.3 = ((bf16[16,12,2048]{2,1,0:T(8,128)(2,1)}), bf16[16,12,2048]{2,1,0:T(8,128)(2,1)S(1)}, u32[]{:S(2)}, u32[]{:S(2)}) async-start(bf16[16,12,2048]{2,1,0:T(8,128)(2,1)} %reshape.50), calls=%async_computation.3 | async-start | bytes 2097152 | tf_op jit(solution)/shard_map/all_to_all | solution.py:88
  254.5 22.9 %all-to-all-done.3 = bf16[16,12,2048]{2,1,0:T(8,128)(2,1)S(1)} async-done(((bf16[16,12,2048]{2,1,0:T(8,128)(2,1)}), bf16[16,12,2048]{2,1,0:T(8,128)(2,1)S(1)}, u32[]{:S(2)}, u32[]{:S(2)}) %all-to-all-start.3) | async-done | bytes 786464 | tf_op jit(solution)/shard_map/all_to_all | solution.py:88
  277.4 0.2 reshape.51
  277.6 0.9 gather_fusion
  278.5 1.1 multiply_convert_fusion.1
  (15 shorter events, 0.2 us)
Async XLA Ops:
  12.3 30.3 %all-to-all-start = ((bf16[16,12,2048]{2,1,0:T(8,128)(2,1)}), bf16[16,12,2048]{2,1,0:T(8,128)(2,1)S(1)}, u32[]{:S(2)}, u32[]{:S(2)}) async-start(bf16[16,12,2048]{2,1,0:T(8,128)(2,1)} %reshape.43), calls=%async_computation | async-start | bytes 2097152 | tf_op jit(solution)/shard_map/all_to_all | solution.py:78
  42.6 29.8 %all-to-all-start.1 = ((bf16[16,12,2048]{2,1,0:T(8,128)(2,1)}), bf16[16,12,2048]{2,1,0:T(8,128)(2,1)S(1)}, u32[]{:S(2)}, u32[]{:S(2)}) async-start(bf16[16,12,2048]{2,1,0:T(8,128)(2,1)} %reshape.45), calls=%async_computation.1 | async-start | bytes 2097152 | tf_op jit(solution)/shard_map/all_to_all | solution.py:79
  49.5 175.9 %all-gather.3.cloned.1.call-start = ((), (), s32[]{:S(2)}) async-start(), calls=%async_computation.4 | async-start | bytes 17825792 | tf_op jit(solution)/shard_map/all_gather | solution.py:14
  77.8 46.4 %all-to-all-start.2 = ((bf16[16,12,2048]{2,1,0:T(8,128)(2,1)}), bf16[16,12,2048]{2,1,0:T(8,128)(2,1)S(1)}, u32[]{:S(2)}, u32[]{:S(2)}) async-start(bf16[16,12,2048]{2,1,0:T(8,128)(2,1)} %reshape.47), calls=%async_computation.2 | async-start | bytes 2097152 | tf_op jit(solution)/shard_map/all_to_all | solution.py:77
  225.5 1.4 copy-start
  228.9 25.5 %copy-start.2 = (s32[128]{0:T(128)S(1)}, s32[128]{0:T(128)}, u32[]{:S(2)}) copy-start(s32[128]{0:T(128)} %param.14) | copy-start | bytes 1540
  228.9 25.5 %copy-start.1 = (f32[3,2048]{1,0:T(4,128)S(1)}, f32[3,2048]{1,0:T(4,128)}, u32[]{:S(2)}) copy-start(f32[3,2048]{1,0:T(4,128)} %param.15) | copy-start | bytes 73732
  230.4 47.0 %all-to-all-start.3 = ((bf16[16,12,2048]{2,1,0:T(8,128)(2,1)}), bf16[16,12,2048]{2,1,0:T(8,128)(2,1)S(1)}, u32[]{:S(2)}, u32[]{:S(2)}) async-start(bf16[16,12,2048]{2,1,0:T(8,128)(2,1)} %reshape.50), calls=%async_computation.3 | async-start | bytes 2097152 | tf_op jit(solution)/shard_map/all_to_all | solution.py:88
Sparse Core Ops, SparseCore 0:
  74.6 150.7 all-gather.2
where the time goes:
time: 289 us; the launch traced here: 286 us
  waiting for transfers between devices  190 us (66%)
  starting transfers between devices  45.2 us (16%)
  local copies, waits for them, and re-layouts  20.2 us (7%)
  between operations  13.6 us (5%)
  matrix products  10.2 us (4%)
  other arithmetic  4.66 us (2%)
    all_gather x1, waiting for transfers between devices, entering(): gathered = lax.all_gather(part, axis)  86.5 us
    all_to_all x1, waiting for transfers between devices, on_device(): lax.all_to_all(q_send, 'seq', split_axis=0, concat_axis=0, tiled=True)  38.2 us
    all_to_all x1, starting transfers between devices, on_device(): lax.all_to_all(normed.reshape(peer_count, capacity, row_width), 'seq', sp...  24 us
    all_to_all x1, waiting for transfers between devices, on_device(): lax.all_to_all(normed.reshape(peer_count, capacity, row_width), 'seq', sp...  22.9 us
    all_to_all x1, waiting for transfers between devices, on_device(): lax.all_to_all(v_send, 'seq', split_axis=0, concat_axis=0, tiled=True)  22.3 us
    all_to_all x1, waiting for transfers between devices, on_device(): lax.all_to_all(k_send, 'seq', split_axis=0, concat_axis=0, tiled=True)  19.7 us
    dot_general x4, matrix products, one_group(): jnp.einsum('hrs,she->rhe', weights, value_group, preferred_element_type=j...  8.36 us
    all_to_all x1, starting transfers between devices, on_device(): lax.all_to_all(k_send, 'seq', split_axis=0, concat_axis=0, tiled=True)  7.39 us
  transfers between devices with their start and end apart: 5, of which 5 were waited for; matrix products, arithmetic and copies ran while one was open for 7% of the time, Pallas kernels for 0%

commit v1 on v0

v1 whole, which is shorter than its diff:
```python
import functools
import math

import jax
import jax.numpy as jnp
from jax import lax
from jax.experimental import pallas as pl
from jax.experimental.pallas import tpu as pltpu
from jax.sharding import PartitionSpec as P

HEADS = 16
HEAD_DIM = 128
QUERY_TILE = 256


def partner(place, distance, count):
    total, bit = 0, 1
    while bit < count:
        total = total + lax.rem(lax.div(place, bit) + lax.div(distance, bit), 2) * bit
        bit *= 2
    return total


def heads_kernel(
    count, q_ref, k_ref, v_ref, key_ref, out_ref,
    q_all, k_all, v_all, key_all, key_col, total, result,
    send_sem, recv_sem, local_sem,
):
    rows = q_ref.shape[0]
    width = q_all.shape[1]
    me = lax.axis_index("seq")

    def at_rows(place):
        return pl.ds(pl.multiple_of(place * rows, rows), rows)

    def at_columns(place):
        return pl.ds(pl.multiple_of(place * width, width), width)

    def outgoing(kind, distance):
        other = partner(me, distance, count)
        if kind == 3:
            source, target = key_ref, key_all.at[me]
        elif kind == 4:
            source, target = result.at[at_rows(other)], out_ref.at[:, at_columns(me)]
        else:
            source = (q_ref, k_ref, v_ref)[kind].at[:, at_columns(other)]
            target = (q_all, k_all, v_all)[kind].at[at_rows(me)]
        return pltpu.make_async_remote_copy(
            src_ref=source, dst_ref=target,
            send_sem=send_sem.at[kind, distance], recv_sem=recv_sem.at[kind, distance],
            device_id={"seq": other}, device_id_type=pl.DeviceIdType.MESH,
        )

    def incoming(kind, distance):
        other = partner(me, distance, count)
        if kind == 3:
            source, target = key_ref, key_all.at[other]
        elif kind == 4:
            source, target = result.at[at_rows(other)], out_ref.at[:, at_columns(other)]
        else:
            source = (q_ref, k_ref, v_ref)[kind].at[:, at_columns(other)]
            target = (q_all, k_all, v_all)[kind].at[at_rows(other)]
        return pltpu.make_async_remote_copy(
            src_ref=source, dst_ref=target,
            send_sem=send_sem.at[kind, distance], recv_sem=recv_sem.at[kind, distance],
            device_id={"seq": other}, device_id_type=pl.DeviceIdType.MESH,
        )

    barrier = pltpu.get_barrier_semaphore()

    def greet(step, _):
        pl.semaphore_signal(
            barrier, inc=1, device_id={"seq": partner(me, step + 1, count)},
            device_id_type=pl.DeviceIdType.MESH,
        )
        return 0

    lax.fori_loop(0, count - 1, greet, 0)

    own = [
        pltpu.make_async_copy(src.at[:, at_columns(me)], dst.at[at_rows(me)], local_sem.at[kind])
        for kind, (src, dst) in enumerate(((q_ref, q_all), (k_ref, k_all), (v_ref, v_all)))
    ] + [pltpu.make_async_copy(key_ref, key_all.at[me], local_sem.at[3])]
    for copy in own:
        copy.start()
    total[...] = jnp.zeros_like(total)
    pl.semaphore_wait(barrier, count - 1)

    def send_first(step, _):
        outgoing(3, count - 1 - step).start()
        outgoing(0, count - 1 - step).start()
        return 0

    def send_second(step, _):
        outgoing(1, count - 1 - step).start()
        outgoing(2, count - 1 - step).start()
        return 0

    lax.fori_loop(0, count - 1, send_first, 0)
    lax.fori_loop(0, count - 1, send_second, 0)
    for copy in own:
        copy.wait()

    def place_keys(place):
        line = jnp.broadcast_to(key_all[place][0:1], (rows, rows))
        key_col[at_rows(place), :] = line.T

    place_keys(me)

    def arrive(step, _):
        distance = count - 1 - step
        incoming(3, distance).wait_recv()
        place_keys(partner(me, distance, count))
        incoming(0, distance).wait_recv()
        return 0

    lax.fori_loop(0, count - 1, arrive, 0)

    tokens = q_all.shape[0]
    tile = math.gcd(tokens, QUERY_TILE)

    def attend(place):
        line = key_all[place][0:1]
        for head in range(width // HEAD_DIM):
            lanes = slice(head * HEAD_DIM, (head + 1) * HEAD_DIM)
            keys = k_all[at_rows(place), lanes]
            values = v_all[at_rows(place), lanes]
            for start in range(0, tokens, tile):
                part = slice(start, start + tile)
                scores = lax.dot_general(
                    q_all[part, lanes], keys, (((1,), (1,)), ((), ())),
                    preferred_element_type=jnp.float32,
                )
                weights = jnp.where(key_col[part, :] >= line, scores, 0.0).astype(jnp.bfloat16)
                total[part, lanes] += jnp.dot(weights, values, preferred_element_type=jnp.float32)

    def one_source(step, _):
        distance = count - step

        @pl.when(step > 0)
        def _():
            incoming(1, distance).wait_recv()
            incoming(2, distance).wait_recv()

        attend(partner(me, lax.rem(distance, count), count))
        return 0

    lax.fori_loop(0, count, one_source, 0)

    def finish(place):
        for head in range(width // HEAD_DIM):
            lanes = slice(head * HEAD_DIM, (head + 1) * HEAD_DIM)
            combined = total[at_rows(place), lanes]
            scale = lax.rsqrt(jnp.mean(combined * combined, axis=-1, keepdims=True) + 1e-06)
            result[at_rows(place), lanes] = (combined * scale).astype(jnp.bfloat16)

    def give_back(step, _):
        distance = count - 1 - step
        finish(partner(me, distance, count))
        outgoing(4, distance).start()
        return 0

    lax.fori_loop(0, count - 1, give_back, 0)
    finish(me)
    last = pltpu.make_async_copy(result.at[at_rows(me)], out_ref.at[:, at_columns(me)], local_sem.at[0])
    last.start()
    last.wait()

    def settle(step, _):
        distance = count - 1 - step
        for kind in range(5):
            outgoing(kind, distance).wait_send()
        incoming(4, distance).wait_recv()
        return 0

    lax.fori_loop(0, count - 1, settle, 0)


def attend_by_heads(q_rows, k_rows, v_rows, block_of):
    rows, row_width = q_rows.shape
    count = lax.axis_size("seq")
    tokens = rows * count
    width = row_width // count
    place = lax.axis_index("seq") * rows + jnp.arange(rows, dtype=jnp.int32)
    key = (block_of[:, 0] * tokens + place).astype(jnp.float32)
    key = jnp.broadcast_to(key[None, :], (8, rows))
    vmem = pl.BlockSpec(memory_space=pltpu.VMEM)
    shared = pltpu.VMEM((tokens, width), q_rows.dtype)
    return pl.pallas_call(
        functools.partial(heads_kernel, count),
        out_shape=jax.ShapeDtypeStruct((rows, row_width), q_rows.dtype),
        in_specs=[vmem] * 4,
        out_specs=vmem,
        scratch_shapes=[
            shared, shared, shared,
            pltpu.VMEM((count, 8, rows), jnp.float32),
            pltpu.VMEM((tokens, rows), jnp.float32),
            pltpu.VMEM((tokens, width), jnp.float32),
            shared,
            pltpu.SemaphoreType.DMA((5, count)),
            pltpu.SemaphoreType.DMA((5, count)),
            pltpu.SemaphoreType.DMA((4,)),
        ],
        compiler_params=pltpu.CompilerParams(
            collective_id=0, has_side_effects=True, vmem_limit_bytes=40 * 2**20
        ),
        cost_estimate=pl.CostEstimate(
            flops=4 * tokens * tokens * width, bytes_accessed=8 * rows * row_width, transcendentals=tokens
        ),
    )(q_rows, k_rows, v_rows, key)


def entering(part, axis):
    place = lax.axis_index(axis)
    count = lax.axis_size(axis)
    state = lax.ppermute(part, axis, [(i, i + 1) for i in range(count - 1)])
    reach = 1
    while reach < count:
        state = state + lax.ppermute(state, axis, [(i, i + reach) for i in range(count - reach)])
        reach *= 2
    return state


def block_state(key_rows, value_rows):
    return jnp.einsum("shd,she->hde", key_rows, value_rows, preferred_element_type=jnp.float32)


def attend(queries, row_order, key_rows, value_rows, carried):
    row_count = queries.shape[0]
    head_count = queries.shape[1]
    slot_count = key_rows.shape[0]
    group_size = math.gcd(head_count, 4)
    carried_part = jnp.einsum("rhd,hde->rhe", queries, carried, preferred_element_type=jnp.float32)
    causal = row_order[:, None] >= jnp.arange(slot_count, dtype=jnp.int32)[None, :]

    def one_group(group_id):
        query_group = lax.dynamic_slice_in_dim(queries, group_id * group_size, group_size, 1)
        key_group = lax.dynamic_slice_in_dim(key_rows, group_id * group_size, group_size, 1)
        value_group = lax.dynamic_slice_in_dim(value_rows, group_id * group_size, group_size, 1)
        scores = jnp.einsum(
            "rhd,shd->hrs", query_group, key_group, preferred_element_type=jnp.float32
        )
        weights = jnp.where(causal[None], scores, 0.0).astype(jnp.bfloat16)
        return jnp.einsum("hrs,she->rhe", weights, value_group, preferred_element_type=jnp.float32)

    pieces = lax.map(one_group, jnp.arange(head_count // group_size, dtype=jnp.int32))
    local_part = jnp.moveaxis(pieces, 0, 1).reshape(row_count, head_count, queries.shape[2])
    combined = carried_part + local_part
    scale = lax.rsqrt(jnp.mean(combined * combined, axis=-1, keepdims=True) + 1e-06)
    return (combined * scale).astype(jnp.bfloat16)


def attend_by_blocks(q_rows, k_rows, v_rows, block_of):
    tok_count = q_rows.shape[0]
    row_width = q_rows.shape[1]
    peer_count = lax.axis_size("seq")
    capacity = max(2, 3 * tok_count // (2 * peer_count))
    slot_count = peer_count * capacity
    target = block_of[:, 0]
    place = jnp.arange(tok_count, dtype=jnp.int32)
    earlier_same = (target[:, None] == target[None, :]) & (place[None, :] < place[:, None])
    slot_rank = jnp.sum(earlier_same.astype(jnp.int32), axis=1)
    slot_index = target * capacity + slot_rank

    def routed(row_block):
        buffer = jnp.zeros((slot_count, row_width), row_block.dtype).at[slot_index].set(row_block)
        moved = lax.all_to_all(
            buffer.reshape(peer_count, capacity, row_width), "seq", split_axis=0, concat_axis=0, tiled=True
        )
        return moved.reshape(slot_count, HEADS, HEAD_DIM)

    queries, key_rows, value_rows = routed(q_rows), routed(k_rows), routed(v_rows)
    prefix = entering(block_state(key_rows, value_rows), "seq")
    carried = prefix.astype(jnp.bfloat16)
    normed = attend(queries, jnp.arange(slot_count, dtype=jnp.int32), key_rows, value_rows, carried)
    returned = lax.all_to_all(
        normed.reshape(peer_count, capacity, row_width), "seq", split_axis=0, concat_axis=0, tiled=True
    )
    return returned.reshape(slot_count, row_width)[slot_index]


def on_device(q_rows, k_rows, v_rows, block_of, modality, out_gain):
    count = lax.axis_size("seq")
    plan = attend_by_heads if count > 1 and HEADS % count == 0 else attend_by_blocks
    own_rows = plan(q_rows, k_rows, v_rows, block_of)
    chosen = modality[:, None]
    gains = jnp.where(
        chosen == 0,
        out_gain[0][None, :],
        jnp.where(chosen == 1, out_gain[1][None, :], out_gain[2][None, :]),
    )
    return (own_rows.astype(jnp.float32) * gains).astype(jnp.bfloat16)


def solution(mesh):
    placed = (
        P(("groups", "seq"), None),
        P(("groups", "seq"), None),
        P(("groups", "seq"), None),
        P(("groups", "seq"), None),
        P(("groups", "seq")),
        P(),
    )
    return jax.shard_map(
        on_device, mesh=mesh, in_specs=placed, out_specs=P(("groups", "seq"), None), check_vma=False
    )
```

time: 289 us -> 66 us (0.23)
  waiting for transfers between devices: 190 us -> 0 us
  Pallas kernels: 0 us -> 60.1 us
  starting transfers between devices: 45.2 us -> 0 us
  local copies, waits for them, and re-layouts: 20.2 us -> 4.46 us
  between operations: 13.6 us -> 0.04 us
  matrix products: 10.2 us -> 0 us
  other arithmetic: 4.66 us -> 1.07 us
    all_to_all x4 -> x0, waiting for transfers between devices: 103 us -> none  [the longest x1 38.2 us: on_device(): lax.all_to_all(q_send, 'seq', split_axis=0, concat_axis=0, tiled=True)]
    all_gather x1 -> x0, waiting for transfers between devices: 86.5 us -> none  [entering(): gathered = lax.all_gather(part, axis)]
    pallas_call x0 -> x1, Pallas kernels: none -> 60.1 us  [attend_by_heads(): pl.pallas_call(functools.partial(heads_kernel, count), out_shape=jax.Shap...]
    all_to_all x4 -> x0, starting transfers between devices: 45.1 us -> none  [the longest x1 24 us: on_device(): lax.all_to_all(normed.reshape(peer_count, capacity, row_width), 'seq', sp...]
    dot_general x6 -> x0, matrix products: 10.2 us -> none  [the longest x4 8.36 us: one_group(): jnp.einsum('hrs,she->rhe', weights, value_group, preferred_element_type=j...]
    reshape x11 -> x0, local copies, waits for them, and re-layouts: 8.32 us -> none  [the longest x3 3.51 us: packed(): return buffer.reshape(peer_count, capacity, row_width)]
    scatter x3 -> x0, local copies, waits for them, and re-layouts: 6.33 us -> none  [packed(): jnp.zeros((slot_count, row_width), row_block.dtype).at[slot_index]]
    unnamed x6 -> x12, local copies, waits for them, and re-layouts: 1.4 us -> 4.43 us
  transfers between devices with their start and end apart: 5 -> 0, of which waited for: 5 -> 0; matrix products, arithmetic and copies ran while one was open for 7% -> 0% of each run, Pallas kernels for 0% -> 0%
where the time goes in v1:
time: 66 us; the launch traced here: 65.7 us
  Pallas kernels  60.1 us (91%)
  local copies, waits for them, and re-layouts  4.46 us (7%)
  other arithmetic  1.07 us (2%)
    pallas_call x1, Pallas kernels, attend_by_heads(): pl.pallas_call(functools.partial(heads_kernel, count), out_shape=jax.Shap...  60.1 us
    unnamed x12, local copies, waits for them, and re-layouts  4.43 us

profile of v1, /device:TPU:0, one launch (start us, length us, event | category | flops | bytes accessed | tf_op | source)
XLA Modules:
  0.0 65.7 jit_solution(16294094723465308325)
XLA Ops:
  0.0 0.0 copy-start.4
  0.0 0.7 copy-done.4
  0.7 0.0 copy-start
  0.7 1.0 %copy-done = bf16[128,2048]{1,0:T(8,128)(2,1)S(1)} copy-done((bf16[128,2048]{1,0:T(8,128)(2,1)S(1)}, bf16[128,2048]{1,0:T(8,128)(2,1)}, u32[]{:S(2)}) %copy-start) | copy-done | bytes 524312
  1.7 0.0 copy-start.1
  1.7 1.0 %copy-done.1 = bf16[128,2048]{1,0:T(8,128)(2,1)S(1)} copy-done((bf16[128,2048]{1,0:T(8,128)(2,1)S(1)}, bf16[128,2048]{1,0:T(8,128)(2,1)}, u32[]{:S(2)}) %copy-start.1) | copy-done | bytes 524312
  2.8 0.0 copy-start.2
  2.8 1.0 %copy-done.2 = bf16[128,2048]{1,0:T(8,128)(2,1)S(1)} copy-done((bf16[128,2048]{1,0:T(8,128)(2,1)S(1)}, bf16[128,2048]{1,0:T(8,128)(2,1)}, u32[]{:S(2)}) %copy-start.2) | copy-done | bytes 524312
  3.8 0.0 copy-start.3
  3.8 60.1 %shard_map.64 = bf16[128,2048]{1,0:T(8,128)(2,1)S(1)} custom-call(bf16[128,2048]{1,0:T(8,128)(2,1)S(1)} %copy-done, bf16[128,2048]{1,0:T(8,128)(2,1)S(1)} %copy-done.1, bf16[128,2048]{1,0:T(8,128)(2,1)S(1)} %copy-done.2, f32[8,128]{1,0:T(8,128)S(1)} %broadcast_in_dim.53.key_ref), custom_call_target="tpu_custom_call" | custom-call | flops 2147483648 | bytes 2097152 | tf_op jit(solution)/shard_map/pallas_call | solution.py:189
  63.9 0.0 copy-done.3
  64.0 0.0 copy-start.5
  64.0 0.6 copy-done.5
  64.6 1.1 %multiply_convert_fusion = bf16[128,2048]{1,0:T(8,128)(2,1)} fusion(bf16[128,2048]{1,0:T(8,128)(2,1)S(1)} %shard_map.64, f32[2048]{0:T(1024)S(1)} %bitcast.8, f32[2048]{0:T(1024)S(1)} %bitcast.9, f32[2048]{0:T(1024)S(1)} %bitcast.7, pred[128]{0:T(512)(128)(4,1)S(1)} %get-tuple-element.9, pred[128]{0:T(512)(128)(4,1)S(1)} %get-tuple-element.8), kind=kLoop, calls=%fused_computation | loop fusion | flops 1310720 | bytes 1073408 | tf_op jit(solution)/shard_map/convert_element_type | solution.py:292
  (4 shorter events, 0.0 us)
Async XLA Ops:
  0.0 0.7 copy-start.4
  0.7 1.0 %copy-start = (bf16[128,2048]{1,0:T(8,128)(2,1)S(1)}, bf16[128,2048]{1,0:T(8,128)(2,1)}, u32[]{:S(2)}) copy-start(bf16[128,2048]{1,0:T(8,128)(2,1)} %q_ref.1) | copy-start | bytes 1572868
  1.7 1.0 %copy-start.1 = (bf16[128,2048]{1,0:T(8,128)(2,1)S(1)}, bf16[128,2048]{1,0:T(8,128)(2,1)}, u32[]{:S(2)}) copy-start(bf16[128,2048]{1,0:T(8,128)(2,1)} %k_ref.1) | copy-start | bytes 1572868
  2.8 1.0 %copy-start.2 = (bf16[128,2048]{1,0:T(8,128)(2,1)S(1)}, bf16[128,2048]{1,0:T(8,128)(2,1)}, u32[]{:S(2)}) copy-start(bf16[128,2048]{1,0:T(8,128)(2,1)} %v_ref.1) | copy-start | bytes 1572868
  3.8 60.1 %copy-start.3 = (f32[3,2048]{1,0:T(4,128)S(1)}, f32[3,2048]{1,0:T(4,128)}, u32[]{:S(2)}) copy-start(f32[3,2048]{1,0:T(4,128)} %param.11) | copy-start | bytes 73732
  64.0 0.7 %copy-start.5 = (s32[128]{0:T(128)S(1)}, s32[128]{0:T(128)}, u32[]{:S(2)}) copy-start(s32[128]{0:T(128)} %param.10) | copy-start | bytes 1540

commit v2 on v1

v2 whole, which is shorter than its diff:
```python
import functools
import math

import jax
import jax.numpy as jnp
from jax import lax
from jax.experimental import pallas as pl
from jax.experimental.pallas import tpu as pltpu
from jax.sharding import PartitionSpec as P

HEADS = 16
HEAD_DIM = 128
BLOCK_ROWS = 16


def partner(place, distance, count):
    total, bit = 0, 1
    while bit < count:
        total = total + lax.rem(lax.div(place, bit) + lax.div(distance, bit), 2) * bit
        bit *= 2
    return total


def heads_kernel(
    count, q_hbm, k_hbm, v_hbm, block_hbm, out_ref,
    raw, raw_block, outbox, inbox, key_line, key_col, total, result,
    send_sem, recv_sem, local_sem,
):
    rows = raw.shape[1]
    width = inbox.shape[2]
    first = rows + BLOCK_ROWS
    tokens = total.shape[0]
    pairs = count // 2
    me = lax.axis_index("seq")
    parts = (slice(0, first), slice(first, first + 2 * rows))

    def at_rows(place, size):
        return pl.ds(pl.multiple_of(place * size, size), size)

    def across(kind, distance, sending):
        other = partner(me, distance, count)
        at, at_out = (me, me) if sending else (other, other)
        if kind == 2:
            source, target = result.at[at_rows(other, rows)], out_ref.at[:, at_rows(at_out, width)]
        else:
            source, target = outbox.at[other, parts[kind]], inbox.at[at, parts[kind]]
        return pltpu.make_async_remote_copy(
            src_ref=source, dst_ref=target,
            send_sem=send_sem.at[kind, distance], recv_sem=recv_sem.at[kind, distance],
            device_id={"seq": other}, device_id_type=pl.DeviceIdType.MESH,
        )

    load = [
        pltpu.make_async_copy(src, raw.at[kind], local_sem.at[kind])
        for kind, src in enumerate((q_hbm, k_hbm, v_hbm))
    ]
    load_block = pltpu.make_async_copy(block_hbm, raw_block, local_sem.at[3])
    load_block.start()
    for copy in load:
        copy.start()

    barrier = pltpu.get_barrier_semaphore()

    def greet(step, _):
        pl.semaphore_signal(
            barrier, inc=1, device_id={"seq": partner(me, step + 1, count)},
            device_id_type=pl.DeviceIdType.MESH,
        )
        return 0

    lax.fori_loop(0, count - 1, greet, 0)

    def sort_out(kind, start):
        load[kind].wait()
        for other in range(count):
            outbox[other, start:start + rows, :] = raw[kind, :, other * width:(other + 1) * width]

    def far_first(step):
        return lax.rem(count - step, count)

    load_block.wait()
    blocks = jnp.broadcast_to(raw_block[...].astype(jnp.float32), (BLOCK_ROWS, rows)).astype(outbox.dtype)
    for other in range(count):
        outbox[other, rows:first, 0:rows] = blocks
    sort_out(0, 0)
    pl.semaphore_wait(barrier, count - 1)

    def send(kind):
        def one(step, _):
            across(kind, far_first(step + 1), True).start()
            return 0

        lax.fori_loop(0, count - 1, one, 0)

    send(0)
    sort_out(1, first)
    sort_out(2, first + rows)
    send(1)
    own = pltpu.make_async_copy(outbox.at[me], inbox.at[me], local_sem.at[3])
    own.start()
    total[...] = jnp.zeros_like(total)
    own.wait()

    def place_keys(place):
        block = inbox[place, rows:first, 0:rows][0:1].astype(jnp.float32)
        row = lax.broadcasted_iota(jnp.int32, (1, rows), 1) + place * rows
        line = block * tokens + row.astype(jnp.float32)
        key_line[:, at_rows(place, rows)] = jnp.broadcast_to(line, (8, rows))
        key_col[at_rows(place, rows), :] = jnp.broadcast_to(line, (rows, rows)).T

    place_keys(me)

    def arrive(step, _):
        distance = far_first(step + 1)
        across(0, distance, False).wait_recv()
        place_keys(partner(me, distance, count))
        return 0

    lax.fori_loop(0, count - 1, arrive, 0)

    def both(pair, start, lanes):
        return inbox[pl.ds(2 * pair, 2), start:start + rows, lanes].reshape(2 * rows, HEAD_DIM)

    def attended(query_pair, key_pair, lanes):
        scores = lax.dot_general(
            both(query_pair, 0, lanes), both(key_pair, first, lanes), (((1,), (1,)), ((), ())),
            preferred_element_type=jnp.float32,
        )
        column = key_col[at_rows(query_pair, 2 * rows), :]
        line = key_line[0:1, at_rows(key_pair, 2 * rows)]
        causal = jnp.concatenate([column >= line[:, :rows], column >= line[:, rows:]], axis=1)
        weights = jnp.where(causal, scores, 0.0).astype(jnp.bfloat16)
        return jnp.dot(weights, both(key_pair, first + rows, lanes), preferred_element_type=jnp.float32)

    shares = [slice(start, start + HEAD_DIM) for start in range(0, width, HEAD_DIM)]

    def wait_pair(distance):
        across(1, 2 * distance + 1, False).wait_recv()

        @pl.when(distance > 0)
        def _():
            across(1, 2 * distance, False).wait_recv()

    def one_pair(step, _):
        distance = lax.rem(pairs - step, pairs)
        wait_pair(distance)
        key_pair = partner(lax.div(me, 2), distance, pairs)
        for lanes in shares:
            for query_pair in range(pairs):
                total[query_pair * 2 * rows:(query_pair + 1) * 2 * rows, lanes] += attended(
                    query_pair, key_pair, lanes
                )
        return 0

    lax.fori_loop(1, pairs, one_pair, 0)
    wait_pair(0)

    def finish(step, _):
        distance = lax.rem(2 * pairs - 1 - step, pairs)
        query_pair = partner(lax.div(me, 2), distance, pairs)
        at = at_rows(query_pair, 2 * rows)
        for lanes in shares:
            combined = total[at, lanes] + attended(query_pair, lax.div(me, 2), lanes)
            scale = lax.rsqrt(jnp.mean(combined * combined, axis=-1, keepdims=True) + 1e-06)
            result[at, lanes] = (combined * scale).astype(jnp.bfloat16)
        across(2, 2 * distance + 1, True).start()

        @pl.when(distance > 0)
        def _():
            across(2, 2 * distance, True).start()

        return 0

    lax.fori_loop(0, pairs, finish, 0)
    last = pltpu.make_async_copy(
        result.at[at_rows(me, rows)], out_ref.at[:, at_rows(me, width)], local_sem.at[3]
    )
    last.start()
    last.wait()

    def settle(step, _):
        distance = far_first(step + 1)
        for kind in range(3):
            across(kind, distance, True).wait_send()
        across(2, distance, False).wait_recv()
        return 0

    lax.fori_loop(0, count - 1, settle, 0)


def attend_by_heads(q_rows, k_rows, v_rows, block_of):
    rows, row_width = q_rows.shape
    count = lax.axis_size("seq")
    tokens = rows * count
    width = row_width // count
    anywhere = pl.BlockSpec(memory_space=pl.ANY)
    message = pltpu.VMEM((count, 3 * rows + BLOCK_ROWS, width), q_rows.dtype)
    return pl.pallas_call(
        functools.partial(heads_kernel, count),
        out_shape=jax.ShapeDtypeStruct((rows, row_width), q_rows.dtype),
        in_specs=[anywhere] * 4,
        out_specs=pl.BlockSpec(memory_space=pltpu.VMEM),
        scratch_shapes=[
            pltpu.VMEM((3, rows, row_width), q_rows.dtype),
            pltpu.VMEM((1, rows), jnp.int32),
            message,
            message,
            pltpu.VMEM((8, tokens), jnp.float32),
            pltpu.VMEM((tokens, rows), jnp.float32),
            pltpu.VMEM((tokens, width), jnp.float32),
            pltpu.VMEM((tokens, width), q_rows.dtype),
            pltpu.SemaphoreType.DMA((3, count)),
            pltpu.SemaphoreType.DMA((3, count)),
            pltpu.SemaphoreType.DMA((4,)),
        ],
        compiler_params=pltpu.CompilerParams(
            collective_id=0, has_side_effects=True, vmem_limit_bytes=56 * 2**20
        ),
        cost_estimate=pl.CostEstimate(
            flops=4 * tokens * tokens * width, bytes_accessed=8 * rows * row_width, transcendentals=tokens
        ),
    )(q_rows, k_rows, v_rows, block_of.reshape(1, rows))


def entering(part, axis):
    place = lax.axis_index(axis)
    count = lax.axis_size(axis)
    state = lax.ppermute(part, axis, [(i, i + 1) for i in range(count - 1)])
    reach = 1
    while reach < count:
        state = state + lax.ppermute(state, axis, [(i, i + reach) for i in range(count - reach)])
        reach *= 2
    return state


def block_state(key_rows, value_rows):
    return jnp.einsum("shd,she->hde", key_rows, value_rows, preferred_element_type=jnp.float32)


def attend(queries, row_order, key_rows, value_rows, carried):
    row_count = queries.shape[0]
    head_count = queries.shape[1]
    slot_count = key_rows.shape[0]
    group_size = math.gcd(head_count, 4)
    carried_part = jnp.einsum("rhd,hde->rhe", queries, carried, preferred_element_type=jnp.float32)
    causal = row_order[:, None] >= jnp.arange(slot_count, dtype=jnp.int32)[None, :]

    def one_group(group_id):
        query_group = lax.dynamic_slice_in_dim(queries, group_id * group_size, group_size, 1)
        key_group = lax.dynamic_slice_in_dim(key_rows, group_id * group_size, group_size, 1)
        value_group = lax.dynamic_slice_in_dim(value_rows, group_id * group_size, group_size, 1)
        scores = jnp.einsum(
            "rhd,shd->hrs", query_group, key_group, preferred_element_type=jnp.float32
        )
        weights = jnp.where(causal[None], scores, 0.0).astype(jnp.bfloat16)
        return jnp.einsum("hrs,she->rhe", weights, value_group, preferred_element_type=jnp.float32)

    pieces = lax.map(one_group, jnp.arange(head_count // group_size, dtype=jnp.int32))
    local_part = jnp.moveaxis(pieces, 0, 1).reshape(row_count, head_count, queries.shape[2])
    combined = carried_part + local_part
    scale = lax.rsqrt(jnp.mean(combined * combined, axis=-1, keepdims=True) + 1e-06)
    return (combined * scale).astype(jnp.bfloat16)


def attend_by_blocks(q_rows, k_rows, v_rows, block_of):
    tok_count = q_rows.shape[0]
    row_width = q_rows.shape[1]
    peer_count = lax.axis_size("seq")
    capacity = max(2, 3 * tok_count // (2 * peer_count))
    slot_count = peer_count * capacity
    target = block_of[:, 0]
    place = jnp.arange(tok_count, dtype=jnp.int32)
    earlier_same = (target[:, None] == target[None, :]) & (place[None, :] < place[:, None])
    slot_rank = jnp.sum(earlier_same.astype(jnp.int32), axis=1)
    slot_index = target * capacity + slot_rank

    def routed(row_block):
        buffer = jnp.zeros((slot_count, row_width), row_block.dtype).at[slot_index].set(row_block)
        moved = lax.all_to_all(
            buffer.reshape(peer_count, capacity, row_width), "seq", split_axis=0, concat_axis=0, tiled=True
        )
        return moved.reshape(slot_count, HEADS, HEAD_DIM)

    queries, key_rows, value_rows = routed(q_rows), routed(k_rows), routed(v_rows)
    prefix = entering(block_state(key_rows, value_rows), "seq")
    carried = prefix.astype(jnp.bfloat16)
    normed = attend(queries, jnp.arange(slot_count, dtype=jnp.int32), key_rows, value_rows, carried)
    returned = lax.all_to_all(
        normed.reshape(peer_count, capacity, row_width), "seq", split_axis=0, concat_axis=0, tiled=True
    )
    return returned.reshape(slot_count, row_width)[slot_index]


def on_device(q_rows, k_rows, v_rows, block_of, modality, out_gain):
    rows = q_rows.shape[0]
    count = lax.axis_size("seq")
    by_heads = count > 1 and HEADS % count == 0 and rows == HEAD_DIM
    plan = attend_by_heads if by_heads else attend_by_blocks
    own_rows = plan(q_rows, k_rows, v_rows, block_of)
    chosen = modality[:, None]
    gains = jnp.where(
        chosen == 0,
        out_gain[0][None, :],
        jnp.where(chosen == 1, out_gain[1][None, :], out_gain[2][None, :]),
    )
    return (own_rows.astype(jnp.float32) * gains).astype(jnp.bfloat16)


def solution(mesh):
    placed = (
        P(("groups", "seq"), None),
        P(("groups", "seq"), None),
        P(("groups", "seq"), None),
        P(("groups", "seq"), None),
        P(("groups", "seq")),
        P(),
    )
    return jax.shard_map(
        on_device, mesh=mesh, in_specs=placed, out_specs=P(("groups", "seq"), None), check_vma=False
    )
```

time: 66 us -> 62.5 us (0.947)
  local copies, waits for them, and re-layouts: 4.46 us -> 1.55 us
  Pallas kernels: 60.1 us -> 58.6 us
  other arithmetic: 1.07 us -> 2.1 us
    unnamed x12 -> x2, local copies, waits for them, and re-layouts: 4.43 us -> 0.65 us
    pallas_call x1, Pallas kernels: 60.1 us -> 58.6 us  [attend_by_heads(): pl.pallas_call(functools.partial(heads_kernel, count), out_shape=jax.Shap...]
    convert_element_type x1, other arithmetic: 1.06 us -> 2.1 us  [on_device(): return (own_rows.astype(jnp.float32) * gains).astype(jnp.bfloat16)]
    slice x1, local copies, waits for them, and re-layouts: 0.02 us -> 0.89 us  [on_device(): out_gain[0][None, :]]
where the time goes in v2:
time: 62.5 us; the launch traced here: 62.2 us
  Pallas kernels  58.6 us (94%)
  other arithmetic  2.1 us (3%)
  local copies, waits for them, and re-layouts  1.55 us (2%)
    pallas_call x1, Pallas kernels, attend_by_heads(): pl.pallas_call(functools.partial(heads_kernel, count), out_shape=jax.Shap...  58.6 us
    convert_element_type x1, other arithmetic, on_device(): return (own_rows.astype(jnp.float32) * gains).astype(jnp.bfloat16)  2.1 us

profile of v2, /device:TPU:0, one launch (start us, length us, event | category | flops | bytes accessed | tf_op | source)
XLA Modules:
  0.0 62.2 jit_solution(17327089412084252570)
XLA Ops:
  0.0 0.0 copy-start
  0.0 0.7 %copy-done = s32[128]{0:T(128)S(1)} copy-done((s32[128]{0:T(128)S(1)}, s32[128]{0:T(128)}, u32[]{:S(2)}) %copy-start) | copy-done | bytes 536
  0.7 0.9 %fusion = (f32[1,2048]{1,0:T(1,128)S(1)}, f32[1,2048]{1,0:T(1,128)S(1)}, f32[1,2048]{1,0:T(1,128)S(1)}) fusion(f32[3,2048]{1,0:T(4,128)} %param.11), kind=kLoop, calls=%fused_computation.3 | loop fusion | bytes 49152 | tf_op jit(solution)/shard_map/slice | solution.py:303
  1.6 58.6 %shard_map.64 = bf16[128,2048]{1,0:T(8,128)(2,1)} custom-call(bf16[128,2048]{1,0:T(8,128)(2,1)} %q_hbm.1, bf16[128,2048]{1,0:T(8,128)(2,1)} %k_hbm.1, bf16[128,2048]{1,0:T(8,128)(2,1)} %v_hbm.1, s32[1,128]{1,0:T(1,128)} %bitcast.7), custom_call_target="tpu_custom_call" | custom-call | flops 2147483648 | bytes 2097152 | tf_op jit(solution)/shard_map/pallas_call | solution.py:198
  60.1 2.1 %multiply_convert_fusion = bf16[128,2048]{1,0:T(8,128)(2,1)} fusion(bf16[128,2048]{1,0:T(8,128)(2,1)} %shard_map.64, f32[2048]{0:T(1024)S(1)} %bitcast.5, f32[2048]{0:T(1024)S(1)} %bitcast.6, f32[2048]{0:T(1024)S(1)} %bitcast.4, pred[128]{0:T(512)(128)(4,1)S(1)} %get-tuple-element.9, pred[128]{0:T(512)(128)(4,1)S(1)} %get-tuple-element.8), kind=kLoop, calls=%fused_computation | loop fusion | flops 1310720 | bytes 1073408 | tf_op jit(solution)/shard_map/convert_element_type | solution.py:306
  (1 shorter events, 0.0 us)
Async XLA Ops:
  0.0 0.7 %copy-start = (s32[128]{0:T(128)S(1)}, s32[128]{0:T(128)}, u32[]{:S(2)}) copy-start(s32[128]{0:T(128)} %param.10) | copy-start | bytes 1540

commit v3 on v2

--- a/solution.py
+++ b/solution.py
@@ -11,6 +11,7 @@
 HEADS = 16
 HEAD_DIM = 128
 BLOCK_ROWS = 16
+FAR_WINDOW = 2
 
 
 def partner(place, distance, count):
@@ -22,8 +23,8 @@
 
 
 def heads_kernel(
-    count, q_hbm, k_hbm, v_hbm, block_hbm, out_ref,
-    raw, raw_block, outbox, inbox, key_line, key_col, total, result,
+    count, q_hbm, k_hbm, v_hbm, block_hbm, mode_hbm, gain_hbm, out_ref,
+    raw, raw_block, raw_mode, gains, outbox, inbox, key_line, key_col, mode_col, total, result, back,
     send_sem, recv_sem, local_sem,
 ):
     rows = raw.shape[1]
@@ -39,9 +40,9 @@
 
     def across(kind, distance, sending):
         other = partner(me, distance, count)
-        at, at_out = (me, me) if sending else (other, other)
+        at = me if sending else other
         if kind == 2:
-            source, target = result.at[at_rows(other, rows)], out_ref.at[:, at_rows(at_out, width)]
+            source, target = result.at[at_rows(other, rows)], back.at[at]
         else:
             source, target = outbox.at[other, parts[kind]], inbox.at[at, parts[kind]]
         return pltpu.make_async_remote_copy(
@@ -55,8 +56,9 @@
         for kind, src in enumerate((q_hbm, k_hbm, v_hbm))
     ]
     load_block = pltpu.make_async_copy(block_hbm, raw_block, local_sem.at[3])
-    load_block.start()
-    for copy in load:
+    load_mode = pltpu.make_async_copy(mode_hbm, raw_mode, local_sem.at[4])
+    load_gain = pltpu.make_async_copy(gain_hbm, gains, local_sem.at[5])
+    for copy in (load_block, *load, load_mode, load_gain):
         copy.start()
 
     barrier = pltpu.get_barrier_semaphore()
@@ -85,20 +87,40 @@
     sort_out(0, 0)
     pl.semaphore_wait(barrier, count - 1)
 
-    def send(kind):
-        def one(step, _):
-            across(kind, far_first(step + 1), True).start()
-            return 0
-
-        lax.fori_loop(0, count - 1, one, 0)
-
-    send(0)
+    near = pairs // 2
+    far = pairs - near
+    window = min(FAR_WINDOW, far)
+
+    def send_first(step, _):
+        across(0, far_first(step + 1), True).start()
+        return 0
+
+    def send_pair(distance):
+        across(1, 2 * distance + 1, True).start()
+
+        @pl.when(distance > 0)
+        def _():
+            across(1, 2 * distance, True).start()
+
+    def send_near(distance, _):
+        send_pair(distance)
+        return 0
+
+    def send_far(step, _):
+        send_pair(pairs - 1 - step)
+        return 0
+
+    lax.fori_loop(0, count - 1, send_first, 0)
     sort_out(1, first)
     sort_out(2, first + rows)
-    send(1)
+    lax.fori_loop(0, window, send_far, 0)
+    lax.fori_loop(0, near, send_near, 0)
     own = pltpu.make_async_copy(outbox.at[me], inbox.at[me], local_sem.at[3])
     own.start()
     total[...] = jnp.zeros_like(total)
+    load_mode.wait()
+    load_gain.wait()
+    mode_col[...] = jnp.broadcast_to(raw_mode[...].astype(jnp.float32), (rows, rows)).T
     own.wait()
 
     def place_keys(place):
@@ -141,26 +163,40 @@
         def _():
             across(1, 2 * distance, False).wait_recv()
 
-    def one_pair(step, _):
-        distance = lax.rem(pairs - step, pairs)
-        wait_pair(distance)
+    def take_keys(distance):
         key_pair = partner(lax.div(me, 2), distance, pairs)
         for lanes in shares:
             for query_pair in range(pairs):
                 total[query_pair * 2 * rows:(query_pair + 1) * 2 * rows, lanes] += attended(
                     query_pair, key_pair, lanes
                 )
-        return 0
-
-    lax.fori_loop(1, pairs, one_pair, 0)
-    wait_pair(0)
+
+    def take_near(distance, _):
+        wait_pair(distance)
+        take_keys(distance)
+        return 0
+
+    def take_far(step, _):
+        wait_pair(pairs - 1 - step)
+
+        @pl.when(step < far - window)
+        def _():
+            send_pair(pairs - 1 - step - window)
+
+        take_keys(pairs - 1 - step)
+        return 0
+
+    lax.fori_loop(0, near, take_near, 0)
+    lax.fori_loop(0, far - 1, take_far, 0)
+    wait_pair(near + me * 0)
+    last_pair = partner(lax.div(me, 2), near, pairs)
 
     def finish(step, _):
-        distance = lax.rem(2 * pairs - 1 - step, pairs)
+        distance = pairs - 1 - step
         query_pair = partner(lax.div(me, 2), distance, pairs)
         at = at_rows(query_pair, 2 * rows)
         for lanes in shares:
-            combined = total[at, lanes] + attended(query_pair, lax.div(me, 2), lanes)
+            combined = total[at, lanes] + attended(query_pair, last_pair, lanes)
             scale = lax.rsqrt(jnp.mean(combined * combined, axis=-1, keepdims=True) + 1e-06)
             result[at, lanes] = (combined * scale).astype(jnp.bfloat16)
         across(2, 2 * distance + 1, True).start()
@@ -172,23 +208,32 @@
         return 0
 
     lax.fori_loop(0, pairs, finish, 0)
-    last = pltpu.make_async_copy(
-        result.at[at_rows(me, rows)], out_ref.at[:, at_rows(me, width)], local_sem.at[3]
-    )
-    last.start()
-    last.wait()
+
+    def scaled(source, place):
+        for start in range(0, width, HEAD_DIM):
+            at = pl.ds(pl.multiple_of(place * width + start, HEAD_DIM), HEAD_DIM)
+            gain = jnp.where(
+                mode_col[...] == 0.0, gains[0:1, at],
+                jnp.where(mode_col[...] == 1.0, gains[1:2, at], gains[2:3, at]),
+            )
+            normed = source[:, start:start + HEAD_DIM].astype(jnp.float32)
+            out_ref[:, at] = (normed * gain).astype(out_ref.dtype)
+
+    scaled(result.at[at_rows(me, rows)], me)
 
     def settle(step, _):
-        distance = far_first(step + 1)
+        distance = step + 1
         for kind in range(3):
             across(kind, distance, True).wait_send()
         across(2, distance, False).wait_recv()
+        other = partner(me, distance, count)
+        scaled(back.at[other], other)
         return 0
 
     lax.fori_loop(0, count - 1, settle, 0)
 
 
-def attend_by_heads(q_rows, k_rows, v_rows, block_of):
+def attend_by_heads(q_rows, k_rows, v_rows, block_of, modality, out_gain):
     rows, row_width = q_rows.shape
     count = lax.axis_size("seq")
     tokens = rows * count
@@ -198,20 +243,24 @@
     return pl.pallas_call(
         functools.partial(heads_kernel, count),
         out_shape=jax.ShapeDtypeStruct((rows, row_width), q_rows.dtype),
-        in_specs=[anywhere] * 4,
+        in_specs=[anywhere] * 6,
         out_specs=pl.BlockSpec(memory_space=pltpu.VMEM),
         scratch_shapes=[
             pltpu.VMEM((3, rows, row_width), q_rows.dtype),
             pltpu.VMEM((1, rows), jnp.int32),
+            pltpu.VMEM((1, rows), jnp.int32),
+            pltpu.VMEM(out_gain.shape, jnp.float32),
             message,
             message,
             pltpu.VMEM((8, tokens), jnp.float32),
             pltpu.VMEM((tokens, rows), jnp.float32),
+            pltpu.VMEM((rows, rows), jnp.float32),
             pltpu.VMEM((tokens, width), jnp.float32),
             pltpu.VMEM((tokens, width), q_rows.dtype),
+            pltpu.VMEM((count, rows, width), q_rows.dtype),
             pltpu.SemaphoreType.DMA((3, count)),
             pltpu.SemaphoreType.DMA((3, count)),
-            pltpu.SemaphoreType.DMA((4,)),
+            pltpu.SemaphoreType.DMA((6,)),
         ],
         compiler_params=pltpu.CompilerParams(
             collective_id=0, has_side_effects=True, vmem_limit_bytes=56 * 2**20
@@ -219,7 +268,7 @@
         cost_estimate=pl.CostEstimate(
             flops=4 * tokens * tokens * width, bytes_accessed=8 * rows * row_width, transcendentals=tokens
         ),
-    )(q_rows, k_rows, v_rows, block_of.reshape(1, rows))
+    )(q_rows, k_rows, v_rows, block_of.reshape(1, rows), modality.reshape(1, rows), out_gain)
 
 
 def entering(part, axis):
@@ -262,7 +311,7 @@
     return (combined * scale).astype(jnp.bfloat16)
 
 
-def attend_by_blocks(q_rows, k_rows, v_rows, block_of):
+def attend_by_blocks(q_rows, k_rows, v_rows, block_of, modality, out_gain):
     tok_count = q_rows.shape[0]
     row_width = q_rows.shape[1]
     peer_count = lax.axis_size("seq")
@@ -288,15 +337,7 @@
     returned = lax.all_to_all(
         normed.reshape(peer_count, capacity, row_width), "seq", split_axis=0, concat_axis=0, tiled=True
     )
-    return returned.reshape(slot_count, row_width)[slot_index]
-
-
-def on_device(q_rows, k_rows, v_rows, block_of, modality, out_gain):
-    rows = q_rows.shape[0]
-    count = lax.axis_size("seq")
-    by_heads = count > 1 and HEADS % count == 0 and rows == HEAD_DIM
-    plan = attend_by_heads if by_heads else attend_by_blocks
-    own_rows = plan(q_rows, k_rows, v_rows, block_of)
+    own_rows = returned.reshape(slot_count, row_width)[slot_index]
     chosen = modality[:, None]
     gains = jnp.where(
         chosen == 0,
@@ -304,6 +345,14 @@
         jnp.where(chosen == 1, out_gain[1][None, :], out_gain[2][None, :]),
     )
     return (own_rows.astype(jnp.float32) * gains).astype(jnp.bfloat16)
+
+
+def on_device(q_rows, k_rows, v_rows, block_of, modality, out_gain):
+    rows = q_rows.shape[0]
+    count = lax.axis_size("seq")
+    by_heads = count > 1 and HEADS % count == 0 and rows == HEAD_DIM
+    plan = attend_by_heads if by_heads else attend_by_blocks
+    return plan(q_rows, k_rows, v_rows, block_of, modality, out_gain)
 
 
 def solution(mesh):

time: 62.5 us -> 58.9 us (0.942)
  other arithmetic: 2.1 us -> 0 us
  Pallas kernels: 58.6 us -> 56.8 us
    convert_element_type x1 -> x0, other arithmetic: 2.1 us -> none  [on_device(): return (own_rows.astype(jnp.float32) * gains).astype(jnp.bfloat16)]
    pallas_call x1, Pallas kernels: 58.6 us -> 56.8 us  [attend_by_heads(): pl.pallas_call(functools.partial(heads_kernel, count), out_shape=jax.Shap...]
    unnamed x2 -> x1, local copies, waits for them, and re-layouts: 0.65 us -> 1.88 us
    slice x1 -> x0, local copies, waits for them, and re-layouts: 0.89 us -> none  [on_device(): out_gain[0][None, :]]
where the time goes in v3:
time: 58.9 us; the launch traced here: 58.7 us
  Pallas kernels  56.8 us (96%)
  local copies, waits for them, and re-layouts  1.88 us (3%)
    pallas_call x1, Pallas kernels, attend_by_heads(): pl.pallas_call(functools.partial(heads_kernel, count), out_shape=jax.Shap...  56.8 us
    unnamed x1, local copies, waits for them, and re-layouts  1.88 us

profile of v3, /device:TPU:0, one launch (start us, length us, event | category | flops | bytes accessed | tf_op | source)
XLA Modules:
  0.0 58.7 jit_solution(2574287208443693429)
XLA Ops:
  0.0 56.8 %shard_map.64 = bf16[128,2048]{1,0:T(8,128)(2,1)} custom-call(bf16[128,2048]{1,0:T(8,128)(2,1)} %q_hbm.1, bf16[128,2048]{1,0:T(8,128)(2,1)} %k_hbm.1, bf16[128,2048]{1,0:T(8,128)(2,1)} %v_hbm.1, s32[1,128]{1,0:T(1,128)} %bitcast.2, s32[1,128]{1,0:T(1,128)} %bitcast.3, f32[3,2048]{1,0:T(4,128)} %gain_hbm.1), custom_call_target="tpu_custom_call" | custom-call | flops 2147483648 | bytes 2097152 | tf_op jit(solution)/shard_map/pallas_call | solution.py:243
  56.8 1.9 %copy.8 = bf16[128,2048]{1,0:T(8,128)(2,1)} copy(bf16[128,2048]{1,0:T(8,128)(2,1)} %shard_map.64) | data formatting | bytes 1048576

commit v4 on v3

--- a/solution.py
+++ b/solution.py
@@ -10,7 +10,6 @@
 
 HEADS = 16
 HEAD_DIM = 128
-BLOCK_ROWS = 16
 FAR_WINDOW = 2
 
 
@@ -24,12 +23,12 @@
 
 def heads_kernel(
     count, q_hbm, k_hbm, v_hbm, block_hbm, mode_hbm, gain_hbm, out_ref,
-    raw, raw_block, raw_mode, gains, outbox, inbox, key_line, key_col, mode_col, total, result, back,
+    raw, raw_block, raw_mode, gains, outbox, inbox, blocks, key_line, key_col, mode_col, total, result, back,
     send_sem, recv_sem, local_sem,
 ):
     rows = raw.shape[1]
     width = inbox.shape[2]
-    first = rows + BLOCK_ROWS
+    first = rows
     tokens = total.shape[0]
     pairs = count // 2
     me = lax.axis_index("seq")
@@ -43,6 +42,8 @@
         at = me if sending else other
         if kind == 2:
             source, target = result.at[at_rows(other, rows)], back.at[at]
+        elif kind == 3:
+            source, target = raw_block, blocks.at[at]
         else:
             source, target = outbox.at[other, parts[kind]], inbox.at[at, parts[kind]]
         return pltpu.make_async_remote_copy(
@@ -81,9 +82,6 @@
         return lax.rem(count - step, count)
 
     load_block.wait()
-    blocks = jnp.broadcast_to(raw_block[...].astype(jnp.float32), (BLOCK_ROWS, rows)).astype(outbox.dtype)
-    for other in range(count):
-        outbox[other, rows:first, 0:rows] = blocks
     sort_out(0, 0)
     pl.semaphore_wait(barrier, count - 1)
 
@@ -92,6 +90,7 @@
     window = min(FAR_WINDOW, far)
 
     def send_first(step, _):
+        across(3, far_first(step + 1), True).start()
         across(0, far_first(step + 1), True).start()
         return 0
 
@@ -117,6 +116,7 @@
     lax.fori_loop(0, near, send_near, 0)
     own = pltpu.make_async_copy(outbox.at[me], inbox.at[me], local_sem.at[3])
     own.start()
+    blocks[me] = raw_block[...]
     total[...] = jnp.zeros_like(total)
     load_mode.wait()
     load_gain.wait()
@@ -124,7 +124,7 @@
     own.wait()
 
     def place_keys(place):
-        block = inbox[place, rows:first, 0:rows][0:1].astype(jnp.float32)
+        block = blocks[place].astype(jnp.float32)
         row = lax.broadcasted_iota(jnp.int32, (1, rows), 1) + place * rows
         line = block * tokens + row.astype(jnp.float32)
         key_line[:, at_rows(place, rows)] = jnp.broadcast_to(line, (8, rows))
@@ -134,6 +134,7 @@
 
     def arrive(step, _):
         distance = far_first(step + 1)
+        across(3, distance, False).wait_recv()
         across(0, distance, False).wait_recv()
         place_keys(partner(me, distance, count))
         return 0
@@ -223,7 +224,7 @@
 
     def settle(step, _):
         distance = step + 1
-        for kind in range(3):
+        for kind in range(4):
             across(kind, distance, True).wait_send()
         across(2, distance, False).wait_recv()
         other = partner(me, distance, count)
@@ -239,7 +240,7 @@
     tokens = rows * count
     width = row_width // count
     anywhere = pl.BlockSpec(memory_space=pl.ANY)
-    message = pltpu.VMEM((count, 3 * rows + BLOCK_ROWS, width), q_rows.dtype)
+    message = pltpu.VMEM((count, 3 * rows, width), q_rows.dtype)
     return pl.pallas_call(
         functools.partial(heads_kernel, count),
         out_shape=jax.ShapeDtypeStruct((rows, row_width), q_rows.dtype),
@@ -252,14 +253,15 @@
             pltpu.VMEM(out_gain.shape, jnp.float32),
             message,
             message,
+            pltpu.VMEM((count, 1, rows), jnp.int32),
             pltpu.VMEM((8, tokens), jnp.float32),
             pltpu.VMEM((tokens, rows), jnp.float32),
             pltpu.VMEM((rows, rows), jnp.float32),
             pltpu.VMEM((tokens, width), jnp.float32),
             pltpu.VMEM((tokens, width), q_rows.dtype),
             pltpu.VMEM((count, rows, width), q_rows.dtype),
-            pltpu.SemaphoreType.DMA((3, count)),
-            pltpu.SemaphoreType.DMA((3, count)),
+            pltpu.SemaphoreType.DMA((4, count)),
+            pltpu.SemaphoreType.DMA((4, count)),
             pltpu.SemaphoreType.DMA((6,)),
         ],
         compiler_params=pltpu.CompilerParams(

time: 58.9 us -> 58 us (0.985)
  Pallas kernels: 56.8 us -> 55.9 us
    pallas_call x1, Pallas kernels: 56.8 us -> 55.9 us  [attend_by_heads(): pl.pallas_call(functools.partial(heads_kernel, count), out_shape=jax.Shap...]
where the time goes in v4:
time: 58 us; the launch traced here: 57.8 us
  Pallas kernels  55.9 us (96%)
  local copies, waits for them, and re-layouts  1.88 us (3%)
    pallas_call x1, Pallas kernels, attend_by_heads(): pl.pallas_call(functools.partial(heads_kernel, count), out_shape=jax.Shap...  55.9 us
    unnamed x1, local copies, waits for them, and re-layouts  1.88 us

profile of v4, /device:TPU:0, one launch (start us, length us, event | category | flops | bytes accessed | tf_op | source)
XLA Modules:
  0.0 57.8 jit_solution(5022273434933549612)
XLA Ops:
  0.0 55.9 %shard_map.64 = bf16[128,2048]{1,0:T(8,128)(2,1)} custom-call(bf16[128,2048]{1,0:T(8,128)(2,1)} %q_hbm.1, bf16[128,2048]{1,0:T(8,128)(2,1)} %k_hbm.1, bf16[128,2048]{1,0:T(8,128)(2,1)} %v_hbm.1, s32[1,128]{1,0:T(1,128)} %bitcast.2, s32[1,128]{1,0:T(1,128)} %bitcast.3, f32[3,2048]{1,0:T(4,128)} %gain_hbm.1), custom_call_target="tpu_custom_call" | custom-call | flops 2147483648 | bytes 2097152 | tf_op jit(solution)/shard_map/pallas_call | solution.py:244
  55.9 1.9 %copy.8 = bf16[128,2048]{1,0:T(8,128)(2,1)} copy(bf16[128,2048]{1,0:T(8,128)(2,1)} %shard_map.64) | data formatting | bytes 1048576
